TPU v7x, 128 devices: a whole 4x4x4 slice. The times are simulated.
128 devices in a mesh: sky: 64 (over x, y, z), band: 2 (over core).
Axes of the slice: x: 4, y: 4, z: 4, core: 2. Of those that a mesh axis runs over, the one named last changes fastest.
Arguments:
- stamps: bfloat16 [16384, 6, 2304], P('sky', 'band'), may hold values from 0 to 2
- stamp_gain: bfloat16 [16384], P('sky'), may hold values from 0.5 to 2
- stamp_invvar: bfloat16 [16384], P('sky'), may hold values from 1 to 10
- stamp_dest: int32 [16384, 1], P('sky'), may hold values from 0 to 63; in each aligned block of 256 rows (0 to 255, 256 to 511, ...) at most 8 rows name the same one
- stamp_obj: int32 [16384], P('sky'), may hold values from 0 to 63
- phi_tpl: bfloat16 [6, 16, 2304], P('band'), may hold values from 0 to 0.041503906
- psi_tpl: bfloat16 [6, 16, 2304], P('band'), may hold values from 0 to 0.041503906
- theta_init: float32 [16, 4096], P(None, 'sky'), may hold values from -3 to 3
- nb_id: int32 [4096, 4], P('sky'), may hold values from 0 to 4095, as said below
- nb_weight: float32 [4096, 4], P('sky'), may hold values from 0.2 to 0.8
Outputs:
- theta_fit: float32 [16, 4096], P(None, 'sky')
Inputs may be any that keep to these rules, and one draw needn't show every extreme that they name: `stamp_dest`: among the stamps of one index of sky no destination is named more than 8 times, a bound that some block reaches. `nb_id`: each neighbour is owned by the object's own index of sky or by the index just before or after it, cyclically.
All inputs are finite; a program needn't handle non-finite values.
Results may differ from a plain program's by a relative error of at most 0.0007.
Values may be sent and summed in bfloat16 or wider, within the bound.
A program may use at most 128 MiB of HBM per device.

v0:
```python
import functools

import jax
import jax.numpy as jnp
import numpy as np
from jax import lax
from jax.experimental import pallas as pl
from jax.experimental.pallas import tpu as pltpu
from jax.sharding import PartitionSpec as P

ITERS = 3
CAP = 8
K = 16
ROBUST = 9.0
DAMPING = 0.1
PRIOR = 1.0
STEP_LIMIT = 0.5

MESH = pl.DeviceIdType.MESH
F32 = jnp.float32
BF16 = jnp.bfloat16


def iota(shape, dim):
    return lax.broadcasted_iota(jnp.int32, shape, dim)


def split(x):
    high = x.astype(BF16)
    return high, (x - high.astype(F32)).astype(BF16)


def dot(a, b):
    return jnp.dot(a, b, preferred_element_type=F32)


def dot_t(a, b):
    return lax.dot_general(a, b, (((1,), (1,)), ((), ())), preferred_element_type=F32)


def halves(x):
    width = x.shape[1] // 2
    return x[:, :width] + x[:, width:]


def expand_table():
    table = np.zeros((K * K + K, 384), np.float32)
    for k in range(K):
        for l in range(K):
            a, b = min(k, l), max(k, l)
            if a < 8:
                table[k * K + l, a * K + b] = 1
            elif a == b:
                table[k * K + l, 256 + np.arange(CAP) * K + a - 8] = 1
            else:
                table[k * K + l, (b - 8) * K + a - 8] = 1
        table[K * K + k, 128 + np.arange(CAP) * K + k] = 1
    return table


def solve(full, amp, theta, theta_init):
    sub8 = iota((8, amp.shape[1]), 0)
    amp_lo, amp_hi = amp[:8], amp[8:]
    first, second = [], []
    for k in range(K):
        own = amp[k : k + 1]
        row = full[k * K : k * K + K]
        if k < 8:
            part = row[:8] * (amp_lo * own)
            first.append(part + jnp.where(sub8 == k, DAMPING * part + PRIOR, 0.0))
        else:
            first.append(None)
        part = row[8:] * (amp_hi * own)
        if k >= 8:
            part = part + jnp.where(sub8 == k - 8, DAMPING * part + PRIOR, 0.0)
        second.append(part)
    target = full[K * K :] * amp - PRIOR * (theta - theta_init)
    t0, t1 = target[:8], target[8:]
    ups0, ups1, solved = [], [], []
    for p in range(K):
        r0, r1 = first[p], second[p]
        pivot = r0[p : p + 1] if p < 8 else r1[p - 8 : p - 7]
        inv = 1.0 / pivot
        s0 = None if r0 is None else r0 * inv
        s1 = r1 * inv
        y = (t0[p : p + 1] if p < 8 else t1[p - 8 : p - 7]) * inv
        ups0.append(None if s0 is None else jnp.where(sub8 > p, s0, 0.0))
        ups1.append(jnp.where(sub8 > p - 8, s1, 0.0))
        solved.append(y)
        if r0 is not None:
            t0 = t0 - r0 * y
        t1 = t1 - r1 * y
        for k in range(p + 1, K):
            factor = s0[k : k + 1] if k < 8 else s1[k - 8 : k - 7]
            if k < 8:
                first[k] = first[k] - factor * r0
            second[k] = second[k] - factor * r1
    x0 = jnp.zeros_like(t0)
    x1 = jnp.zeros_like(t1)
    for p in reversed(range(K)):
        known = ups1[p] * x1
        if p < 8:
            known = known + ups0[p] * x0
        value = solved[p] - jnp.sum(known, axis=0, keepdims=True)
        if p < 8:
            x0 = jnp.where(sub8 == p, value, x0)
        else:
            x1 = jnp.where(sub8 == p - 8, value, x1)
    delta = jnp.concatenate([x0, x1], axis=0)
    return theta + STEP_LIMIT * jnp.tanh(delta / STEP_LIMIT)


def kernel(
    dims,
    stamps_ref,
    small_ref,
    nb_ref,
    phi_ref,
    psi_ref,
    theta_ref,
    table_ref,
    out_ref,
    pixels,
    pair,
    wide_phi,
    both,
    gram,
    proj,
    to_slot,
    to_dest,
    from_lit,
    from_near,
    gain_mask,
    plain_mask,
    stamp_cols,
    member,
    member2,
    reply_hi,
    reply_lo,
    theta_now,
    meta_out,
    meta_in,
    nb_in,
    rows_out,
    rows_in,
    reply_out,
    reply_in,
    sums_out,
    sums_in,
    pix_sem,
    meta_send,
    meta_recv,
    nb_send,
    nb_recv,
    rows_send,
    rows_recv,
    reply_send,
    reply_recv,
    sums_send,
    sums_recv,
):
    n_dev, n_stamp, n_obj, pix, chunk = dims
    per_band = pix // chunk
    n_chunk = pixels.shape[0]
    n_slot = n_dev * CAP
    me = lax.axis_index("sky")
    core = lax.axis_index("band")

    def peer(j):
        return lax.rem(me + j, n_dev)

    barrier = pltpu.get_barrier_semaphore()

    def greet(j, carry):
        pl.semaphore_signal(barrier, inc=1, device_id=(peer(j), core), device_id_type=MESH)
        return carry

    lax.fori_loop(1, n_dev, greet, 0)
    pl.semaphore_signal(barrier, inc=1, device_id=(me, 1 - core), device_id_type=MESH)

    pixel_copies = []
    for i in range(n_chunk):
        band, part = divmod(i, per_band)
        copy = pltpu.make_async_copy(
            stamps_ref.at[band, :, pl.ds(part * chunk, chunk)], pixels.at[i], pix_sem.at[i]
        )
        copy.start()
        pixel_copies.append(copy)

    small = small_ref[...]
    cols = jnp.concatenate([small, jnp.zeros((120, n_stamp), F32)], axis=0).T
    gain_row, dest_row, obj_row = small[0:1], small[2:3], small[3:4]
    gain_col, invvar_col, dest_col = cols[:, 0:1], cols[:, 1:2], cols[:, 2:3]
    same = dest_col == dest_row
    low = iota((n_stamp, n_stamp), 0)
    across = iota((n_stamp, n_stamp), 1)
    rank_col = jnp.sum(jnp.where(same & (across < low), 1.0, 0.0), axis=1, keepdims=True)
    rank_row = jnp.sum(jnp.where(same & (low < across), 1.0, 0.0), axis=0, keepdims=True)
    dest_hot = jnp.where(iota((n_dev, n_stamp), 0).astype(F32) == dest_row, 1.0, 0.0).astype(BF16)
    to_dest[...] = dest_hot
    obj_col = cols[:, 3:4]
    named = jnp.where(iota((n_stamp, 128), 1).astype(F32) == rank_col, obj_col + 1.0, 0.0)
    slot_obj = dot(dest_hot, named.astype(BF16))
    meta_out[pl.ds(1, n_dev), 0, :] = slot_obj
    meta_out[0:1, 0, :] = slot_obj[n_dev - 1 :]
    meta_out[n_dev + 1 : n_dev + 2, 0, :] = slot_obj[:1]

    pl.semaphore_wait(barrier, n_dev)

    def send_meta(j, carry):
        t = peer(j)
        pltpu.make_async_remote_copy(
            meta_out.at[pl.ds(t, 3)],
            meta_in.at[:, me],
            meta_send,
            meta_recv,
            device_id=(t, core),
            device_id_type=MESH,
        ).start()
        return carry

    lax.fori_loop(1, n_dev, send_meta, 0)
    nb_copies = []
    for side, step in ((0, 1), (1, n_dev - 1)):
        copy = pltpu.make_async_remote_copy(
            nb_ref,
            nb_in.at[side],
            nb_send.at[side],
            nb_recv.at[side],
            device_id=(peer(step), core),
            device_id_type=MESH,
        )
        copy.start()
        nb_copies.append(copy)
    own_meta = meta_out[pl.ds(me, 3), 0, :]
    meta_in[:, pl.ds(me, 1), 0, :] = own_meta.reshape(3, 1, 128)

    slot_row = dest_row * CAP + rank_row
    to_slot[...] = jnp.where(iota((n_slot, n_stamp), 0).astype(F32) == slot_row, 1.0, 0.0).astype(BF16)
    dest_int = dest_col.astype(jnp.int32)
    owner = iota((n_stamp, n_dev), 1)
    from_lit[...] = jnp.where(owner == dest_int, 1.0, 0.0).astype(BF16)
    shifted = []
    for r in range(3):
        want = dest_int + 1 - r
        want = jnp.where(want < 0, want + n_dev, jnp.where(want >= n_dev, want - n_dev, want))
        shifted.append(jnp.where(owner == want, 1.0, 0.0))
    from_near[...] = jnp.concatenate(shifted, axis=1).astype(BF16)
    group = (iota((n_stamp, 128), 1) // K).astype(F32)
    in_slot = jnp.where(group == rank_col, 1.0, 0.0)
    plain_mask[...] = in_slot
    gain_mask[...] = in_slot * gain_col
    lane = iota((n_stamp, 128), 1)
    stamp_cols[...] = jnp.where(lane == 0, gain_col, jnp.where(lane == 1, ROBUST / invvar_col, 0.0))

    def build(i, carry):
        band = i // per_band
        at = pl.multiple_of((i % per_band) * chunk, chunk)
        phi16 = phi_ref[band, :, pl.ds(at, chunk)]
        phi = phi16.astype(F32)
        swapped = jnp.concatenate([phi[8:], phi[:8]], axis=0)
        sub = iota((K, chunk), 0)
        for k in range(8):
            block = jnp.where(sub >= k, phi * phi[k : k + 1], swapped * phi[8 + k : 9 + k])
            pair[i, k * K : (k + 1) * K, :] = block.astype(BF16)
        rest = (swapped * swapped).astype(BF16)
        for c in range(CAP):
            pair[i, 128 + c * K : 128 + (c + 1) * K, :] = rest
            wide_phi[i, c * K : (c + 1) * K, :] = phi16
        both[i, 0:K, :] = phi16
        both[i, K : 2 * K, :] = psi_ref[band, :, pl.ds(at, chunk)]
        return carry

    for copy in nb_copies:
        copy.wait()
    pltpu.make_async_copy(meta_in.at[:, pl.ds(0, n_dev - 1)], meta_in.at[:, pl.ds(0, n_dev - 1)], meta_recv).wait()
    own_obj = meta_in[1, :, 0, :]
    turned = dot_t(
        jnp.where(iota((128, 128), 0) == iota((128, 128), 1), 1.0, 0.0).astype(BF16), own_obj.astype(BF16)
    )
    spread = dot(
        turned.astype(BF16),
        jnp.where(iota((n_dev, n_slot), 1) // CAP == iota((n_dev, n_slot), 0), 1.0, 0.0).astype(BF16),
    )[:CAP]
    mine = iota((CAP, n_slot), 1) % CAP == iota((CAP, n_slot), 0)
    obj_of_slot = jnp.sum(jnp.where(mine, spread, 0.0), axis=0, keepdims=True)
    member[...] = jnp.where(
        iota((n_obj, n_slot), 0).astype(F32) + 1.0 == obj_of_slot, 1.0, 0.0
    ).astype(BF16)
    obj_sub = iota((n_obj, n_dev), 0).astype(F32) + 1.0
    member2[...] = jnp.concatenate(
        [jnp.where(obj_sub == turned[c : c + 1], 1.0, 0.0) for c in range(CAP)], axis=1
    ).astype(BF16)
    obj_lane = iota((n_dev, n_obj), 1).astype(F32) + 1.0
    reply_hi[0:n_dev, :] = jnp.concatenate(
        [jnp.where(own_obj[:, c : c + 1] == obj_lane, 1.0, 0.0) for c in range(CAP)], axis=1
    ).astype(BF16)
    reply_lo[0:n_dev, :] = jnp.zeros((n_dev, CAP * n_obj), BF16)
    wanted = (iota((n_obj, n_obj), 0) + me * n_obj).astype(F32)
    for r in range(3):
        table = nb_ref[...] if r == 1 else nb_in[0 if r == 0 else 1]
        blend = jnp.zeros((n_obj, n_obj), F32)
        for j in range(4):
            blend = blend + jnp.where(wanted == table[j : j + 1, :n_obj], table[4 + j : 5 + j, :n_obj], 0.0)
        blend_hi, blend_lo = split(blend)
        objects = meta_in[r, :, 0, :]
        his, los = [], []
        for c in range(CAP):
            hot = jnp.where(objects[:, c : c + 1] == obj_lane, 1.0, 0.0).astype(BF16)
            his.append(dot_t(hot, blend_hi))
            los.append(dot_t(hot, blend_lo))
        at = (1 + r) * n_dev
        reply_hi[at : at + n_dev, :] = jnp.concatenate(his, axis=1).astype(BF16)
        reply_lo[at : at + n_dev, :] = jnp.concatenate(los, axis=1).astype(BF16)

    def reply(theta):
        amp = jnp.exp(theta)
        double = jnp.concatenate([amp, amp], axis=1)
        tiled = jnp.concatenate([double] * (CAP // 2), axis=1)
        tiled = jnp.concatenate([tiled] * CAP, axis=0)
        shape = (CAP * K, CAP * n_obj)
        tiled = jnp.where(iota(shape, 0) // K == iota(shape, 1) // n_obj, tiled, 0.0)
        amp_hi, amp_lo = split(tiled)
        answer = (
            dot_t(reply_hi[...], amp_hi) + dot_t(reply_hi[...], amp_lo) + dot_t(reply_lo[...], amp_hi)
        )
        for r in range(4):
            reply_out[r, :, 0, :] = answer[r * n_dev : (r + 1) * n_dev]

        def send(j, carry):
            t = peer(j)
            pltpu.make_async_remote_copy(
                reply_out.at[:, t],
                reply_in.at[:, me],
                reply_send,
                reply_recv,
                device_id=(t, core),
                device_id_type=MESH,
            ).start()
            return carry

        lax.fori_loop(1, n_dev, send, 0)
        reply_in[:, pl.ds(me, 1), 0, :] = reply_out[:, pl.ds(me, 1), 0, :]

    def wait_reply(ref, sem):
        part = ref.at[:, pl.ds(0, n_dev - 1)]
        pltpu.make_async_copy(part, part, sem).wait()

    def wait_rows(ref, sem):
        part = ref.at[pl.ds(0, n_dev - 1)]
        pltpu.make_async_copy(part, part, sem).wait()

    theta_now[...] = theta_ref[...]
    reply(theta_ref[...])
    lax.fori_loop(0, n_chunk, build, 0)
    meta_part = meta_in.at[:, pl.ds(0, n_dev - 1)]
    pltpu.make_async_copy(meta_part, meta_part, meta_send).wait()
    for copy in pixel_copies:
        copy.wait()

    fold_shape = (2 * CAP * K, 2 * K)
    fold_row, fold_col = iota(fold_shape, 0), iota(fold_shape, 1)
    fold = jnp.where(
        (fold_row // (CAP * K) == fold_col // K) & (fold_row % K == fold_col % K), 1.0, 0.0
    ).astype(BF16)

    def sweep(it, carry):
        wait_reply(reply_in, reply_recv)
        lit_hi, lit_lo = split(reply_in[0, :, 0, :])
        near_hi, near_lo = split(jnp.concatenate([reply_in[r, :, 0, :] for r in (1, 2, 3)], axis=0))
        lit = halves(dot(from_lit[...], jnp.concatenate([lit_hi, lit_lo], axis=1)))
        near = halves(dot(from_near[...], jnp.concatenate([near_hi, near_lo], axis=1)))
        wide = jnp.concatenate([lit * gain_mask[...], near * plain_mask[...]], axis=1)
        coeff = dot(wide.astype(BF16), fold).astype(BF16)
        gain = stamp_cols[:, 0:1]
        softening = stamp_cols[:, 1:2]
        gram[...] = jnp.zeros_like(gram)
        proj[...] = jnp.zeros_like(proj)

        def one_chunk(i, carry):
            resid = pixels[i].astype(F32) - dot(coeff, both[i])
            weight = ROBUST / (resid * resid + softening)
            gram[...] += dot_t(weight.astype(BF16), pair[i])
            proj[...] += dot_t((weight * resid).astype(BF16), wide_phi[i])
            return carry

        lax.fori_loop(0, n_chunk, one_chunk, 0)
        square = gain * gain
        main_hi, main_lo = split(gram[:, :128] * square)
        main = halves(dot(to_slot[...], jnp.concatenate([main_hi, main_lo], axis=1)))
        rest = jnp.concatenate(
            [proj[...] * gain_mask[...], gram[:, 128:] * (gain_mask[...] * gain)], axis=1
        )
        rest_hi, rest_lo = split(rest)
        rest = dot(to_dest[...], rest_hi) + dot(to_dest[...], rest_lo)

        @pl.when(it > 0)
        def _():
            wait_rows(rows_out, rows_send)

        rows_out[:, 0:CAP, :] = main.reshape(n_dev, CAP, 128)
        rows_out[:, CAP, :] = rest[:, :128]
        rows_out[:, CAP + 1, :] = rest[:, 128:]

        def send(j, carry):
            t = peer(j)
            pltpu.make_async_remote_copy(
                rows_out.at[t],
                rows_in.at[me],
                rows_send,
                rows_recv,
                device_id=(t, core),
                device_id_type=MESH,
            ).start()
            return carry

        lax.fori_loop(1, n_dev, send, 0)
        rows_in[me] = rows_out[me]

        wait_rows(rows_in, rows_recv)
        slot_hi, slot_lo = split(rows_in[:, 0:CAP, :].reshape(n_slot, 128))
        main_sum = halves(dot(member[...], jnp.concatenate([slot_hi, slot_lo], axis=1)))
        rest = jnp.concatenate([rows_in[:, CAP, :], rows_in[:, CAP + 1, :]], axis=1)
        rest = jnp.concatenate([rest] * CAP, axis=0)
        shape = (CAP * n_dev, 256)
        rest = jnp.where(iota(shape, 0) // n_dev == (iota(shape, 1) % 128) // K, rest, 0.0)
        rest_hi, rest_lo = split(rest)
        rest_sum = dot(member2[...], rest_hi) + dot(member2[...], rest_lo)
        sums = jnp.concatenate([main_sum, rest_sum], axis=1)
        sums_out[it] = sums
        copy = pltpu.make_async_remote_copy(
            sums_out.at[it],
            sums_in.at[it],
            sums_send.at[it],
            sums_recv.at[it],
            device_id=(me, 1 - core),
            device_id_type=MESH,
        )
        copy.start()
        copy.wait()
        sums_hi, sums_lo = split(sums + sums_in[it])
        full = dot_t(table_ref[...], sums_hi) + dot_t(table_ref[...], sums_lo)
        theta = theta_now[...]
        theta = solve(full, jnp.exp(theta), theta, theta_ref[...])
        theta_now[...] = theta
        wait_reply(reply_out, reply_send)

        @pl.when(it < ITERS - 1)
        def _():
            reply(theta)

        return carry

    lax.fori_loop(0, ITERS, sweep, 0)
    wait_rows(rows_out, rows_send)
    out_ref[...] = theta_now[...]


def local(
    stamps,
    stamp_gain,
    stamp_invvar,
    stamp_dest,
    stamp_obj,
    phi_tpl,
    psi_tpl,
    theta_init,
    nb_id,
    nb_weight,
):
    n_dev = lax.axis_size("sky")
    n_stamp, n_band, pix = stamps.shape
    n_obj = theta_init.shape[1]
    chunk = 768 if pix % 768 == 0 else pix
    n_chunk = n_band * (pix // chunk)
    small = jnp.concatenate(
        [
            stamp_gain.astype(F32)[None],
            stamp_invvar.astype(F32)[None],
            stamp_dest[:, 0].astype(F32)[None],
            stamp_obj.astype(F32)[None],
            jnp.zeros((4, n_stamp), F32),
        ],
        axis=0,
    )
    nb = jnp.concatenate([nb_id.T.astype(F32), nb_weight.T], axis=0)
    nb = jnp.pad(nb, ((0, 0), (0, 128 - n_obj)))
    table = jnp.asarray(expand_table(), BF16)
    vmem = pl.BlockSpec(memory_space=pltpu.VMEM)
    n_slot = n_dev * CAP
    scratch = [
        pltpu.VMEM((n_chunk, n_stamp, chunk), BF16),
        pltpu.VMEM((n_chunk, 256, chunk), BF16),
        pltpu.VMEM((n_chunk, 128, chunk), BF16),
        pltpu.VMEM((n_chunk, 32, chunk), BF16),
        pltpu.VMEM((n_stamp, 256), F32),
        pltpu.VMEM((n_stamp, 128), F32),
        pltpu.VMEM((n_slot, n_stamp), BF16),
        pltpu.VMEM((n_dev, n_stamp), BF16),
        pltpu.VMEM((n_stamp, n_dev), BF16),
        pltpu.VMEM((n_stamp, 3 * n_dev), BF16),
        pltpu.VMEM((n_stamp, 128), F32),
        pltpu.VMEM((n_stamp, 128), F32),
        pltpu.VMEM((n_stamp, 128), F32),
        pltpu.VMEM((n_obj, n_slot), BF16),
        pltpu.VMEM((n_obj, n_slot), BF16),
        pltpu.VMEM((4 * n_dev, CAP * n_obj), BF16),
        pltpu.VMEM((4 * n_dev, CAP * n_obj), BF16),
        pltpu.VMEM((K, n_obj), F32),
        pltpu.VMEM((n_dev + 2, 1, 128), F32),
        pltpu.VMEM((3, n_dev, 1, 128), F32),
        pltpu.VMEM((2, 8, 128), F32),
        pltpu.VMEM((n_dev, CAP + 2, 128), F32),
        pltpu.VMEM((n_dev, CAP + 2, 128), F32),
        pltpu.VMEM((4, n_dev, 1, 128), F32),
        pltpu.VMEM((4, n_dev, 1, 128), F32),
        pltpu.VMEM((ITERS, n_obj, 384), F32),
        pltpu.VMEM((ITERS, n_obj, 384), F32),
        pltpu.SemaphoreType.DMA((n_chunk,)),
        pltpu.SemaphoreType.DMA,
        pltpu.SemaphoreType.DMA,
        pltpu.SemaphoreType.DMA((2,)),
        pltpu.SemaphoreType.DMA((2,)),
        pltpu.SemaphoreType.DMA,
        pltpu.SemaphoreType.DMA,
        pltpu.SemaphoreType.DMA,
        pltpu.SemaphoreType.DMA,
        pltpu.SemaphoreType.DMA((ITERS,)),
        pltpu.SemaphoreType.DMA((ITERS,)),
    ]
    return pl.pallas_call(
        functools.partial(kernel, (n_dev, n_stamp, n_obj, pix, chunk)),
        out_shape=jax.ShapeDtypeStruct(theta_init.shape, F32),
        in_specs=[pl.BlockSpec(memory_space=pl.ANY)] + [vmem] * 6,
        out_specs=vmem,
        scratch_shapes=scratch,
        compiler_params=pltpu.CompilerParams(
            collective_id=0, has_side_effects=True, vmem_limit_bytes=50 << 20
        ),
    )(jnp.transpose(stamps, (1, 0, 2)), small, nb, phi_tpl, psi_tpl, theta_init, table)


def solution(mesh):
    in_specs = (
        P("sky", "band", None),
        P("sky"),
        P("sky"),
        P("sky", None),
        P("sky"),
        P("band", None, None),
        P("band", None, None),
        P(None, "sky"),
        P("sky", None),
        P("sky", None),
    )
    out_specs = P(None, "sky")
    return jax.shard_map(local, mesh=mesh, in_specs=in_specs, out_specs=out_specs, check_vma=False)
```

profile of v0, /device:TPU:1, one launch (start us, length us, event | category | flops | bytes accessed | tf_op | source)
XLA Modules:
  0.0 96.4 jit_solution(6870149174060564450)
XLA Ops:
  0.0 0.7 broadcast_in_dim.25
  0.7 0.7 broadcast_in_dim.26
  1.3 0.7 convert_bitcast_fusion.1
  2.0 0.7 convert_element_type.28
  2.7 0.7 convert_bitcast_fusion
  3.4 0.7 select_maximum_fusion.nb_ref
  4.1 0.0 copy-start
  4.1 0.9 copy-done
  5.0 0.0 copy-start.1
  5.0 0.9 copy-done.1
  6.0 0.0 copy-start.2
  6.0 0.9 copy-done.2
  6.9 0.0 copy-start.3
  6.9 0.7 copy-done.3
  7.6 88.2 %shard_map.109 = f32[16,64]{1,0:T(8,128)S(1)} custom-call(bf16[3,256,2304]{2,1,0:T(8,128)(2,1)} %bitcast.9, f32[8,256]{1,0:T(8,128)S(1)} %concatenate.6.small_ref, f32[8,128]{1,0:T(8,128)S(1)} %select_maximum_fusion.nb_ref, bf16[3,16,2304]{2,1,0:T(8,128)(2,1)S(1)} %copy-done, bf16[3,16,2304]{2,1,0:T(8,128)(2,1)S(1)} %copy-done.1, f32[16,64]{1,0:T(8,128)S(1)} %copy-done.3, ...), custom_call_target="tpu_custom_call" | custom-call | tf_op jit(solution)/shard_map/pallas_call | solution.py:531
  95.8 0.6 copy.13
  (2 shorter events, 0.0 us)
Async XLA Ops:
  4.1 0.9 copy-start
  5.0 0.9 copy-start.1
  6.0 0.9 copy-start.2
  6.9 0.7 copy-start.3
where the time goes:
time: 96.7 us; the launch traced here: 96.4 us
  Pallas kernels  88.2 us (91%)
  local copies, waits for them, and re-layouts  4.12 us (4%)
  other arithmetic  4.05 us (4%)
    pallas_call x1, Pallas kernels, local(): pl.pallas_call(functools.partial(kernel, (n_dev, n_stamp, n_obj, pix, chu...  88.2 us
    unnamed x9, local copies, waits for them, and re-layouts  4.09 us

commit v1 on v0

--- a/solution.py
+++ b/solution.py
@@ -56,6 +56,11 @@
                 table[k * K + l, (b - 8) * K + a - 8] = 1
         table[K * K + k, 128 + np.arange(CAP) * K + k] = 1
     return table
+
+
+def offsets(side):
+    steps = [(x, y, z) for x in range(side) for y in range(side) for z in range(side)]
+    return sorted(steps[1:], key=lambda s: -sum(min(d, side - d) for d in s))
 
 
 def solve(full, amp, theta, theta_init):
@@ -113,13 +118,28 @@
 def kernel(
     dims,
     stamps_ref,
-    small_ref,
-    nb_ref,
+    gain_hbm,
+    invvar_hbm,
+    dest_hbm,
+    obj_hbm,
+    phi_hbm,
+    psi_hbm,
+    theta_hbm,
+    nb_id_hbm,
+    nb_weight_hbm,
+    table_hbm,
+    out_ref,
+    gain_ref,
+    invvar_ref,
+    dest_ref,
+    obj_ref,
     phi_ref,
     psi_ref,
     theta_ref,
+    nb_id_ref,
+    nb_weight_ref,
     table_ref,
-    out_ref,
+    nb_ref,
     pixels,
     pair,
     wide_phi,
@@ -147,6 +167,7 @@
     reply_in,
     sums_out,
     sums_in,
+    in_sem,
     pix_sem,
     meta_send,
     meta_recv,
@@ -169,13 +190,48 @@
     def peer(j):
         return lax.rem(me + j, n_dev)
 
+    side = 4
+    x, y, z = me // (side * side), lax.rem(me // side, side), lax.rem(me, side)
+    along_x = [lax.rem(x + d, side) * (side * side) for d in range(side)]
+    along_y = [lax.rem(y + d, side) * side for d in range(side)]
+    along_z = [lax.rem(z + d, side) for d in range(side)]
+
+    def each_peer(act):
+        if n_dev == side**3:
+            for dx, dy, dz in offsets(side):
+                act(along_x[dx] + along_y[dy] + along_z[dz])
+        else:
+
+            def step(j, carry):
+                act(peer(j))
+                return carry
+
+            lax.fori_loop(1, n_dev, step, 0)
+
+    in_copies = []
+    for i, (src, dst) in enumerate(
+        (
+            (gain_hbm, gain_ref),
+            (invvar_hbm, invvar_ref),
+            (dest_hbm, dest_ref),
+            (obj_hbm, obj_ref),
+            (nb_id_hbm, nb_id_ref),
+            (nb_weight_hbm, nb_weight_ref),
+            (theta_hbm, theta_ref),
+            (table_hbm, table_ref),
+            (phi_hbm, phi_ref),
+            (psi_hbm, psi_ref),
+        )
+    ):
+        copy = pltpu.make_async_copy(src, dst, in_sem.at[i])
+        copy.start()
+        in_copies.append(copy)
     barrier = pltpu.get_barrier_semaphore()
 
-    def greet(j, carry):
-        pl.semaphore_signal(barrier, inc=1, device_id=(peer(j), core), device_id_type=MESH)
-        return carry
-
-    lax.fori_loop(1, n_dev, greet, 0)
+    def greet(t):
+        pl.semaphore_signal(barrier, inc=1, device_id=(t, core), device_id_type=MESH)
+
+    each_peer(greet)
     pl.semaphore_signal(barrier, inc=1, device_id=(me, 1 - core), device_id_type=MESH)
 
     pixel_copies = []
@@ -187,7 +243,21 @@
         copy.start()
         pixel_copies.append(copy)
 
-    small = small_ref[...]
+    for copy in in_copies[:8]:
+        copy.wait()
+    small = jnp.concatenate(
+        [
+            gain_ref[...].astype(F32).reshape(1, n_stamp),
+            invvar_ref[...].astype(F32).reshape(1, n_stamp),
+            dest_ref[...].astype(F32).reshape(1, n_stamp),
+            obj_ref[...].astype(F32).reshape(1, n_stamp),
+            jnp.zeros((4, n_stamp), F32),
+        ],
+        axis=0,
+    )
+    nb_ref[...] = jnp.zeros_like(nb_ref)
+    nb_ref[0:4, 0:n_obj] = nb_id_ref[...].astype(F32)
+    nb_ref[4:8, 0:n_obj] = nb_weight_ref[...]
     cols = jnp.concatenate([small, jnp.zeros((120, n_stamp), F32)], axis=0).T
     gain_row, dest_row, obj_row = small[0:1], small[2:3], small[3:4]
     gain_col, invvar_col, dest_col = cols[:, 0:1], cols[:, 1:2], cols[:, 2:3]
@@ -207,8 +277,7 @@
 
     pl.semaphore_wait(barrier, n_dev)
 
-    def send_meta(j, carry):
-        t = peer(j)
+    def send_meta(t):
         pltpu.make_async_remote_copy(
             meta_out.at[pl.ds(t, 3)],
             meta_in.at[:, me],
@@ -217,9 +286,8 @@
             device_id=(t, core),
             device_id_type=MESH,
         ).start()
-        return carry
-
-    lax.fori_loop(1, n_dev, send_meta, 0)
+
+    each_peer(send_meta)
     nb_copies = []
     for side, step in ((0, 1), (1, n_dev - 1)):
         copy = pltpu.make_async_remote_copy(
@@ -327,8 +395,7 @@
         for r in range(4):
             reply_out[r, :, 0, :] = answer[r * n_dev : (r + 1) * n_dev]
 
-        def send(j, carry):
-            t = peer(j)
+        def send(t):
             pltpu.make_async_remote_copy(
                 reply_out.at[:, t],
                 reply_in.at[:, me],
@@ -337,9 +404,8 @@
                 device_id=(t, core),
                 device_id_type=MESH,
             ).start()
-            return carry
-
-        lax.fori_loop(1, n_dev, send, 0)
+
+        each_peer(send)
         reply_in[:, pl.ds(me, 1), 0, :] = reply_out[:, pl.ds(me, 1), 0, :]
 
     def wait_reply(ref, sem):
@@ -352,6 +418,8 @@
 
     theta_now[...] = theta_ref[...]
     reply(theta_ref[...])
+    for copy in in_copies[8:]:
+        copy.wait()
     lax.fori_loop(0, n_chunk, build, 0)
     meta_part = meta_in.at[:, pl.ds(0, n_dev - 1)]
     pltpu.make_async_copy(meta_part, meta_part, meta_send).wait()
@@ -402,8 +470,7 @@
         rows_out[:, CAP, :] = rest[:, :128]
         rows_out[:, CAP + 1, :] = rest[:, 128:]
 
-        def send(j, carry):
-            t = peer(j)
+        def send(t):
             pltpu.make_async_remote_copy(
                 rows_out.at[t],
                 rows_in.at[me],
@@ -412,9 +479,8 @@
                 device_id=(t, core),
                 device_id_type=MESH,
             ).start()
-            return carry
-
-        lax.fori_loop(1, n_dev, send, 0)
+
+        each_peer(send)
         rows_in[me] = rows_out[me]
 
         wait_rows(rows_in, rows_recv)
@@ -471,24 +537,25 @@
     n_dev = lax.axis_size("sky")
     n_stamp, n_band, pix = stamps.shape
     n_obj = theta_init.shape[1]
-    chunk = 768 if pix % 768 == 0 else pix
+    chunk = pix
     n_chunk = n_band * (pix // chunk)
-    small = jnp.concatenate(
-        [
-            stamp_gain.astype(F32)[None],
-            stamp_invvar.astype(F32)[None],
-            stamp_dest[:, 0].astype(F32)[None],
-            stamp_obj.astype(F32)[None],
-            jnp.zeros((4, n_stamp), F32),
-        ],
-        axis=0,
+    table = jnp.asarray(expand_table(), BF16)
+    n_slot = n_dev * CAP
+    operands = (
+        jnp.transpose(stamps, (1, 0, 2)),
+        stamp_gain,
+        stamp_invvar,
+        stamp_dest.reshape(1, n_stamp),
+        stamp_obj.reshape(1, n_stamp),
+        phi_tpl,
+        psi_tpl,
+        theta_init,
+        nb_id.T,
+        nb_weight.T,
+        table,
     )
-    nb = jnp.concatenate([nb_id.T.astype(F32), nb_weight.T], axis=0)
-    nb = jnp.pad(nb, ((0, 0), (0, 128 - n_obj)))
-    table = jnp.asarray(expand_table(), BF16)
-    vmem = pl.BlockSpec(memory_space=pltpu.VMEM)
-    n_slot = n_dev * CAP
-    scratch = [
+    scratch = [pltpu.VMEM(a.shape, a.dtype) for a in operands[1:]] + [
+        pltpu.VMEM((8, 128), F32),
         pltpu.VMEM((n_chunk, n_stamp, chunk), BF16),
         pltpu.VMEM((n_chunk, 256, chunk), BF16),
         pltpu.VMEM((n_chunk, 128, chunk), BF16),
@@ -516,6 +583,7 @@
         pltpu.VMEM((4, n_dev, 1, 128), F32),
         pltpu.VMEM((ITERS, n_obj, 384), F32),
         pltpu.VMEM((ITERS, n_obj, 384), F32),
+        pltpu.SemaphoreType.DMA((10,)),
         pltpu.SemaphoreType.DMA((n_chunk,)),
         pltpu.SemaphoreType.DMA,
         pltpu.SemaphoreType.DMA,
@@ -531,13 +599,13 @@
     return pl.pallas_call(
         functools.partial(kernel, (n_dev, n_stamp, n_obj, pix, chunk)),
         out_shape=jax.ShapeDtypeStruct(theta_init.shape, F32),
-        in_specs=[pl.BlockSpec(memory_space=pl.ANY)] + [vmem] * 6,
-        out_specs=vmem,
+        in_specs=[pl.BlockSpec(memory_space=pltpu.HBM)] * len(operands),
+        out_specs=pl.BlockSpec(memory_space=pltpu.VMEM),
         scratch_shapes=scratch,
         compiler_params=pltpu.CompilerParams(
-            collective_id=0, has_side_effects=True, vmem_limit_bytes=50 << 20
+            collective_id=0, has_side_effects=True, vmem_limit_bytes=(64 << 20) - (1 << 16)
         ),
-    )(jnp.transpose(stamps, (1, 0, 2)), small, nb, phi_tpl, psi_tpl, theta_init, table)
+    )(*operands)
 
 
 def solution(mesh):

time: 96.7 us -> 86.8 us (0.90)
  other arithmetic: 4.05 us -> 0 us
  Pallas kernels: 88.2 us -> 85.3 us
  local copies, waits for them, and re-layouts: 4.12 us -> 1.3 us
    pallas_call x1, Pallas kernels: 88.2 us -> 85.3 us  [local(): pl.pallas_call(functools.partial(kernel, (n_dev, n_stamp, n_obj, pix, chu...]
    unnamed x9 -> x1, local copies, waits for them, and re-layouts: 4.09 us -> 1.3 us
    convert_element_type x3 -> x0, other arithmetic: 2.04 us -> none  [the longest x1 0.68 us: local(): nb = jnp.concatenate([nb_id.T.astype(F32), nb_weight.T], axis=0)]
    broadcast_in_dim x2 -> x0, other arithmetic: 1.31 us -> none  [the longest x1 0.66 us: local(): stamp_invvar.astype(F32)[None]]
where the time goes in v1:
time: 86.8 us; the launch traced here: 86.6 us
  Pallas kernels  85.3 us (98%)
  local copies, waits for them, and re-layouts  1.3 us (1%)
    pallas_call x1, Pallas kernels, local(): pl.pallas_call(functools.partial(kernel, (n_dev, n_stamp, n_obj, pix, chu...  85.3 us

profile of v1, /device:TPU:1, one launch (start us, length us, event | category | flops | bytes accessed | tf_op | source)
XLA Modules:
  0.0 86.6 jit_solution(1914712525039186209)
XLA Ops:
  0.0 85.3 %shard_map.109 = f32[16,64]{1,0:T(8,128)} custom-call(bf16[3,256,2304]{2,1,0:T(8,128)(2,1)} %bitcast.5, bf16[256]{0:T(256)(128)(2,1)} %gain_hbm.1, bf16[256]{0:T(256)(128)(2,1)} %invvar_hbm.1, s32[1,256]{1,0:T(1,128)} %bitcast.8, s32[1,256]{1,0:T(1,128)} %bitcast.9, bf16[3,16,2304]{2,1,0:T(8,128)(2,1)} %phi_hbm.1, bf16[3,16,2304]{2,1,0:T(8,128)(2,1)} %psi_hbm.1, ...), custom_call_target="tpu_custom_call" | custom-call | tf_op jit(solution)/shard_map/pallas_call | solution.py:599
  85.3 1.3 %copy.13 = f32[16,64]{1,0:T(8,128)} copy(f32[16,64]{1,0:T(8,128)} %shard_map.109) | data formatting | bytes 8192

commit v2 on v1

--- a/solution.py
+++ b/solution.py
@@ -28,6 +28,12 @@
 def split(x):
     high = x.astype(BF16)
     return high, (x - high.astype(F32)).astype(BF16)
+
+
+def split3(x):
+    high, rest = x.astype(BF16), x - x.astype(BF16).astype(F32)
+    middle = rest.astype(BF16)
+    return high, middle, (rest - middle.astype(F32)).astype(BF16)
 
 
 def dot(a, b):
@@ -157,6 +163,8 @@
     member2,
     reply_hi,
     reply_lo,
+    reply_mask,
+    amp_parts,
     theta_now,
     meta_out,
     meta_in,
@@ -208,6 +216,14 @@
 
             lax.fori_loop(1, n_dev, step, 0)
 
+    barrier = pltpu.get_barrier_semaphore()
+
+    def greet(t):
+        pl.semaphore_signal(barrier, inc=1, device_id=(t, core), device_id_type=MESH)
+
+    each_peer(greet)
+    pl.semaphore_signal(barrier, inc=1, device_id=(me, 1 - core), device_id_type=MESH)
+
     in_copies = []
     for i, (src, dst) in enumerate(
         (
@@ -226,14 +242,6 @@
         copy = pltpu.make_async_copy(src, dst, in_sem.at[i])
         copy.start()
         in_copies.append(copy)
-    barrier = pltpu.get_barrier_semaphore()
-
-    def greet(t):
-        pl.semaphore_signal(barrier, inc=1, device_id=(t, core), device_id_type=MESH)
-
-    each_peer(greet)
-    pl.semaphore_signal(barrier, inc=1, device_id=(me, 1 - core), device_id_type=MESH)
-
     pixel_copies = []
     for i in range(n_chunk):
         band, part = divmod(i, per_band)
@@ -271,23 +279,12 @@
     obj_col = cols[:, 3:4]
     named = jnp.where(iota((n_stamp, 128), 1).astype(F32) == rank_col, obj_col + 1.0, 0.0)
     slot_obj = dot(dest_hot, named.astype(BF16))
-    meta_out[pl.ds(1, n_dev), 0, :] = slot_obj
-    meta_out[0:1, 0, :] = slot_obj[n_dev - 1 :]
-    meta_out[n_dev + 1 : n_dev + 2, 0, :] = slot_obj[:1]
+    meta_out[1 : n_dev + 1] = slot_obj
+    meta_out[0:1] = slot_obj[n_dev - 1 :]
+    meta_out[n_dev + 1 : n_dev + 2] = slot_obj[:1]
 
     pl.semaphore_wait(barrier, n_dev)
 
-    def send_meta(t):
-        pltpu.make_async_remote_copy(
-            meta_out.at[pl.ds(t, 3)],
-            meta_in.at[:, me],
-            meta_send,
-            meta_recv,
-            device_id=(t, core),
-            device_id_type=MESH,
-        ).start()
-
-    each_peer(send_meta)
     nb_copies = []
     for side, step in ((0, 1), (1, n_dev - 1)):
         copy = pltpu.make_async_remote_copy(
@@ -300,8 +297,19 @@
         )
         copy.start()
         nb_copies.append(copy)
-    own_meta = meta_out[pl.ds(me, 3), 0, :]
-    meta_in[:, pl.ds(me, 1), 0, :] = own_meta.reshape(3, 1, 128)
+    def send_meta(t):
+        pltpu.make_async_remote_copy(
+            meta_out.at[pl.ds(t, 3)],
+            meta_in.at[:, me],
+            meta_send,
+            meta_recv,
+            device_id=(t, core),
+            device_id_type=MESH,
+        ).start()
+
+    each_peer(send_meta)
+    for r in range(3):
+        meta_in[r, pl.ds(me, 1), :] = meta_out[pl.ds(me + r, 1), :]
 
     slot_row = dest_row * CAP + rank_row
     to_slot[...] = jnp.where(iota((n_slot, n_stamp), 0).astype(F32) == slot_row, 1.0, 0.0).astype(BF16)
@@ -339,19 +347,100 @@
         both[i, K : 2 * K, :] = psi_ref[band, :, pl.ds(at, chunk)]
         return carry
 
+    pairs = CAP // 2
+    shape = (CAP * K, CAP * n_obj)
+    reply_mask[...] = jnp.where(iota(shape, 0) // K == iota(shape, 1) // n_obj, 1.0, 0.0).astype(BF16)
+
+    def spread_amp(theta):
+        for part, amp in enumerate(split3(jnp.exp(theta))):
+            double = jnp.concatenate([amp, amp], axis=1)
+            tiled = jnp.concatenate([double] * pairs, axis=1)
+            amp_parts[part] = jnp.concatenate([tiled] * CAP, axis=0) * reply_mask[...]
+
+    spread_amp(theta_ref[...])
+    wanted = (iota((n_obj, n_obj), 0) + me * n_obj).astype(F32)
+
+    def blend_of(table):
+        blend = jnp.zeros((n_obj, n_obj), F32)
+        for j in range(4):
+            blend = blend + jnp.where(wanted == table[j : j + 1, :n_obj], table[4 + j : 5 + j, :n_obj], 0.0)
+        zero = jnp.zeros_like(blend)
+        twice = jnp.concatenate(
+            [jnp.concatenate([blend, zero], axis=1), jnp.concatenate([zero, blend], axis=1)], axis=0
+        )
+        return jnp.concatenate(split(twice), axis=0)
+
+    blends = [None, blend_of(nb_ref[...]), None]
     for copy in nb_copies:
         copy.wait()
-    pltpu.make_async_copy(meta_in.at[:, pl.ds(0, n_dev - 1)], meta_in.at[:, pl.ds(0, n_dev - 1)], meta_recv).wait()
-    own_obj = meta_in[1, :, 0, :]
+    blends[0], blends[2] = blend_of(nb_in[0]), blend_of(nb_in[1])
+    meta_part = meta_in.at[:, pl.ds(0, n_dev - 1)]
+    pltpu.make_async_copy(meta_part, meta_part, meta_recv).wait()
+    lane = iota((n_dev, 2 * n_obj), 1)
+    number = (lane % n_obj).astype(F32) + 1.0
+    for r in range(3):
+        objects = meta_in[r]
+        hots = [
+            jnp.where(
+                jnp.where(lane < n_obj, objects[:, 2 * i : 2 * i + 1], objects[:, 2 * i + 1 : 2 * i + 2]) == number,
+                1.0,
+                0.0,
+            ).astype(BF16)
+            for i in range(pairs)
+        ]
+        if r == 1:
+            reply_hi[0:n_dev, :] = jnp.concatenate(hots, axis=1)
+        weights = dot_t(jnp.concatenate(hots, axis=0), blends[r]).astype(BF16)
+        at = (1 + r) * n_dev
+        for i in range(pairs):
+            own = weights[i * n_dev : (i + 1) * n_dev]
+            columns = slice(i * 2 * n_obj, (i + 1) * 2 * n_obj)
+            reply_hi[at : at + n_dev, columns] = own[:, : 2 * n_obj]
+            reply_lo[at - n_dev : at, columns] = own[:, 2 * n_obj :]
+
+    def reply():
+        for part in range(3):
+            term = dot_t(reply_hi[0:n_dev, :], amp_parts[part])
+            lit = term if part == 0 else lit + term
+        reply_out[0] = lit
+        near = dot_t(reply_hi[n_dev:, :], amp_parts[0]) + dot_t(reply_hi[n_dev:, :], amp_parts[1])
+        near = near + dot_t(reply_lo[...], amp_parts[0])
+        for r in range(3):
+            reply_out[1 + r] = near[r * n_dev : (r + 1) * n_dev]
+
+        def send(t):
+            pltpu.make_async_remote_copy(
+                reply_out.at[:, pl.ds(t, 1)],
+                reply_in.at[:, pl.ds(me, 1)],
+                reply_send,
+                reply_recv,
+                device_id=(t, core),
+                device_id_type=MESH,
+            ).start()
+
+        each_peer(send)
+        reply_in[:, pl.ds(me, 1), :] = reply_out[:, pl.ds(me, 1), :]
+
+    def wait_reply(ref, sem):
+        part = ref.at[:, pl.ds(0, n_dev - 1)]
+        pltpu.make_async_copy(part, part, sem).wait()
+
+    def wait_rows(ref, sem):
+        part = ref.at[pl.ds(0, n_dev - 1)]
+        pltpu.make_async_copy(part, part, sem).wait()
+
+    theta_now[...] = theta_ref[...]
+    reply()
+    own_obj = meta_in[1]
     turned = dot_t(
         jnp.where(iota((128, 128), 0) == iota((128, 128), 1), 1.0, 0.0).astype(BF16), own_obj.astype(BF16)
     )
-    spread = dot(
+    placed = dot(
         turned.astype(BF16),
         jnp.where(iota((n_dev, n_slot), 1) // CAP == iota((n_dev, n_slot), 0), 1.0, 0.0).astype(BF16),
     )[:CAP]
     mine = iota((CAP, n_slot), 1) % CAP == iota((CAP, n_slot), 0)
-    obj_of_slot = jnp.sum(jnp.where(mine, spread, 0.0), axis=0, keepdims=True)
+    obj_of_slot = jnp.sum(jnp.where(mine, placed, 0.0), axis=0, keepdims=True)
     member[...] = jnp.where(
         iota((n_obj, n_slot), 0).astype(F32) + 1.0 == obj_of_slot, 1.0, 0.0
     ).astype(BF16)
@@ -359,69 +448,9 @@
     member2[...] = jnp.concatenate(
         [jnp.where(obj_sub == turned[c : c + 1], 1.0, 0.0) for c in range(CAP)], axis=1
     ).astype(BF16)
-    obj_lane = iota((n_dev, n_obj), 1).astype(F32) + 1.0
-    reply_hi[0:n_dev, :] = jnp.concatenate(
-        [jnp.where(own_obj[:, c : c + 1] == obj_lane, 1.0, 0.0) for c in range(CAP)], axis=1
-    ).astype(BF16)
-    reply_lo[0:n_dev, :] = jnp.zeros((n_dev, CAP * n_obj), BF16)
-    wanted = (iota((n_obj, n_obj), 0) + me * n_obj).astype(F32)
-    for r in range(3):
-        table = nb_ref[...] if r == 1 else nb_in[0 if r == 0 else 1]
-        blend = jnp.zeros((n_obj, n_obj), F32)
-        for j in range(4):
-            blend = blend + jnp.where(wanted == table[j : j + 1, :n_obj], table[4 + j : 5 + j, :n_obj], 0.0)
-        blend_hi, blend_lo = split(blend)
-        objects = meta_in[r, :, 0, :]
-        his, los = [], []
-        for c in range(CAP):
-            hot = jnp.where(objects[:, c : c + 1] == obj_lane, 1.0, 0.0).astype(BF16)
-            his.append(dot_t(hot, blend_hi))
-            los.append(dot_t(hot, blend_lo))
-        at = (1 + r) * n_dev
-        reply_hi[at : at + n_dev, :] = jnp.concatenate(his, axis=1).astype(BF16)
-        reply_lo[at : at + n_dev, :] = jnp.concatenate(los, axis=1).astype(BF16)
-
-    def reply(theta):
-        amp = jnp.exp(theta)
-        double = jnp.concatenate([amp, amp], axis=1)
-        tiled = jnp.concatenate([double] * (CAP // 2), axis=1)
-        tiled = jnp.concatenate([tiled] * CAP, axis=0)
-        shape = (CAP * K, CAP * n_obj)
-        tiled = jnp.where(iota(shape, 0) // K == iota(shape, 1) // n_obj, tiled, 0.0)
-        amp_hi, amp_lo = split(tiled)
-        answer = (
-            dot_t(reply_hi[...], amp_hi) + dot_t(reply_hi[...], amp_lo) + dot_t(reply_lo[...], amp_hi)
-        )
-        for r in range(4):
-            reply_out[r, :, 0, :] = answer[r * n_dev : (r + 1) * n_dev]
-
-        def send(t):
-            pltpu.make_async_remote_copy(
-                reply_out.at[:, t],
-                reply_in.at[:, me],
-                reply_send,
-                reply_recv,
-                device_id=(t, core),
-                device_id_type=MESH,
-            ).start()
-
-        each_peer(send)
-        reply_in[:, pl.ds(me, 1), 0, :] = reply_out[:, pl.ds(me, 1), 0, :]
-
-    def wait_reply(ref, sem):
-        part = ref.at[:, pl.ds(0, n_dev - 1)]
-        pltpu.make_async_copy(part, part, sem).wait()
-
-    def wait_rows(ref, sem):
-        part = ref.at[pl.ds(0, n_dev - 1)]
-        pltpu.make_async_copy(part, part, sem).wait()
-
-    theta_now[...] = theta_ref[...]
-    reply(theta_ref[...])
     for copy in in_copies[8:]:
         copy.wait()
     lax.fori_loop(0, n_chunk, build, 0)
-    meta_part = meta_in.at[:, pl.ds(0, n_dev - 1)]
     pltpu.make_async_copy(meta_part, meta_part, meta_send).wait()
     for copy in pixel_copies:
         copy.wait()
@@ -434,9 +463,9 @@
 
     def sweep(it, carry):
         wait_reply(reply_in, reply_recv)
-        lit_hi, lit_lo = split(reply_in[0, :, 0, :])
-        near_hi, near_lo = split(jnp.concatenate([reply_in[r, :, 0, :] for r in (1, 2, 3)], axis=0))
-        lit = halves(dot(from_lit[...], jnp.concatenate([lit_hi, lit_lo], axis=1)))
+        near_hi, near_lo = split(jnp.concatenate([reply_in[r] for r in (1, 2, 3)], axis=0))
+        lit = dot(from_lit[...], jnp.concatenate(split3(reply_in[0]), axis=1))
+        lit = lit[:, :128] + lit[:, 128:256] + lit[:, 256:]
         near = halves(dot(from_near[...], jnp.concatenate([near_hi, near_lo], axis=1)))
         wide = jnp.concatenate([lit * gain_mask[...], near * plain_mask[...]], axis=1)
         coeff = dot(wide.astype(BF16), fold).astype(BF16)
@@ -445,14 +474,14 @@
         gram[...] = jnp.zeros_like(gram)
         proj[...] = jnp.zeros_like(proj)
 
-        def one_chunk(i, carry):
+        def one_chunk(i):
             resid = pixels[i].astype(F32) - dot(coeff, both[i])
             weight = ROBUST / (resid * resid + softening)
             gram[...] += dot_t(weight.astype(BF16), pair[i])
             proj[...] += dot_t((weight * resid).astype(BF16), wide_phi[i])
-            return carry
-
-        lax.fori_loop(0, n_chunk, one_chunk, 0)
+
+        for i in range(n_chunk):
+            one_chunk(i)
         square = gain * gain
         main_hi, main_lo = split(gram[:, :128] * square)
         main = halves(dot(to_slot[...], jnp.concatenate([main_hi, main_lo], axis=1)))
@@ -513,7 +542,8 @@
 
         @pl.when(it < ITERS - 1)
         def _():
-            reply(theta)
+            spread_amp(theta)
+            reply()
 
         return carry
 
@@ -572,15 +602,17 @@
         pltpu.VMEM((n_obj, n_slot), BF16),
         pltpu.VMEM((n_obj, n_slot), BF16),
         pltpu.VMEM((4 * n_dev, CAP * n_obj), BF16),
-        pltpu.VMEM((4 * n_dev, CAP * n_obj), BF16),
+        pltpu.VMEM((3 * n_dev, CAP * n_obj), BF16),
+        pltpu.VMEM((CAP * K, CAP * n_obj), BF16),
+        pltpu.VMEM((3, CAP * K, CAP * n_obj), BF16),
         pltpu.VMEM((K, n_obj), F32),
-        pltpu.VMEM((n_dev + 2, 1, 128), F32),
-        pltpu.VMEM((3, n_dev, 1, 128), F32),
+        pltpu.VMEM((n_dev + 8, 128), F32),
+        pltpu.VMEM((3, n_dev, 128), F32),
         pltpu.VMEM((2, 8, 128), F32),
         pltpu.VMEM((n_dev, CAP + 2, 128), F32),
         pltpu.VMEM((n_dev, CAP + 2, 128), F32),
-        pltpu.VMEM((4, n_dev, 1, 128), F32),
-        pltpu.VMEM((4, n_dev, 1, 128), F32),
+        pltpu.VMEM((4, n_dev, 128), F32),
+        pltpu.VMEM((4, n_dev, 128), F32),
         pltpu.VMEM((ITERS, n_obj, 384), F32),
         pltpu.VMEM((ITERS, n_obj, 384), F32),
         pltpu.SemaphoreType.DMA((10,)),

time: 86.8 us -> 81.8 us (0.942)
  Pallas kernels: 85.3 us -> 80.3 us
    pallas_call x1, Pallas kernels: 85.3 us -> 80.3 us  [local(): pl.pallas_call(functools.partial(kernel, (n_dev, n_stamp, n_obj, pix, chu...]
where the time goes in v2:
time: 81.8 us; the launch traced here: 81.6 us
  Pallas kernels  80.3 us (98%)
  local copies, waits for them, and re-layouts  1.3 us (2%)
    pallas_call x1, Pallas kernels, local(): pl.pallas_call(functools.partial(kernel, (n_dev, n_stamp, n_obj, pix, chu...  80.3 us

profile of v2, /device:TPU:1, one launch (start us, length us, event | category | flops | bytes accessed | tf_op | source)
XLA Modules:
  0.0 81.6 jit_solution(5684963543715162553)
XLA Ops:
  0.0 80.3 %shard_map.109 = f32[16,64]{1,0:T(8,128)} custom-call(bf16[3,256,2304]{2,1,0:T(8,128)(2,1)} %bitcast.5, bf16[256]{0:T(256)(128)(2,1)} %gain_hbm.1, bf16[256]{0:T(256)(128)(2,1)} %invvar_hbm.1, s32[1,256]{1,0:T(1,128)} %bitcast.8, s32[1,256]{1,0:T(1,128)} %bitcast.9, bf16[3,16,2304]{2,1,0:T(8,128)(2,1)} %phi_hbm.1, bf16[3,16,2304]{2,1,0:T(8,128)(2,1)} %psi_hbm.1, ...), custom_call_target="tpu_custom_call" | custom-call | tf_op jit(solution)/shard_map/pallas_call | solution.py:631
  80.3 1.3 %copy.13 = f32[16,64]{1,0:T(8,128)} copy(f32[16,64]{1,0:T(8,128)} %shard_map.109) | data formatting | bytes 8192

commit v3 on v2

--- a/solution.py
+++ b/solution.py
@@ -118,7 +118,7 @@
         else:
             x1 = jnp.where(sub8 == p - 8, value, x1)
     delta = jnp.concatenate([x0, x1], axis=0)
-    return theta + STEP_LIMIT * jnp.tanh(delta / STEP_LIMIT)
+    return STEP_LIMIT * jnp.tanh(delta / STEP_LIMIT)
 
 
 def kernel(
@@ -148,7 +148,6 @@
     nb_ref,
     pixels,
     pair,
-    wide_phi,
     both,
     gram,
     proj,
@@ -157,6 +156,7 @@
     from_lit,
     from_near,
     gain_mask,
+    gain_rows,
     plain_mask,
     stamp_cols,
     member,
@@ -326,6 +326,8 @@
     in_slot = jnp.where(group == rank_col, 1.0, 0.0)
     plain_mask[...] = in_slot
     gain_mask[...] = in_slot * gain_col
+    in_slot_row = (iota((128, n_stamp), 0) // K).astype(F32) == rank_row
+    gain_rows[...] = jnp.where(in_slot_row, gain_row, 0.0)
     lane = iota((n_stamp, 128), 1)
     stamp_cols[...] = jnp.where(lane == 0, gain_col, jnp.where(lane == 1, ROBUST / invvar_col, 0.0))
 
@@ -342,7 +344,6 @@
         rest = (swapped * swapped).astype(BF16)
         for c in range(CAP):
             pair[i, 128 + c * K : 128 + (c + 1) * K, :] = rest
-            wide_phi[i, c * K : (c + 1) * K, :] = phi16
         both[i, 0:K, :] = phi16
         both[i, K : 2 * K, :] = psi_ref[band, :, pl.ds(at, chunk)]
         return carry
@@ -368,7 +369,7 @@
         twice = jnp.concatenate(
             [jnp.concatenate([blend, zero], axis=1), jnp.concatenate([zero, blend], axis=1)], axis=0
         )
-        return jnp.concatenate(split(twice), axis=0)
+        return jnp.concatenate(split3(twice), axis=0)
 
     blends = [None, blend_of(nb_ref[...]), None]
     for copy in nb_copies:
@@ -396,15 +397,18 @@
             own = weights[i * n_dev : (i + 1) * n_dev]
             columns = slice(i * 2 * n_obj, (i + 1) * 2 * n_obj)
             reply_hi[at : at + n_dev, columns] = own[:, : 2 * n_obj]
-            reply_lo[at - n_dev : at, columns] = own[:, 2 * n_obj :]
+            reply_lo[0, at - n_dev : at, columns] = own[:, 2 * n_obj : 4 * n_obj]
+            reply_lo[1, at - n_dev : at, columns] = own[:, 4 * n_obj :]
 
     def reply():
         for part in range(3):
             term = dot_t(reply_hi[0:n_dev, :], amp_parts[part])
             lit = term if part == 0 else lit + term
         reply_out[0] = lit
-        near = dot_t(reply_hi[n_dev:, :], amp_parts[0]) + dot_t(reply_hi[n_dev:, :], amp_parts[1])
-        near = near + dot_t(reply_lo[...], amp_parts[0])
+        tables = (reply_hi[n_dev:, :], reply_lo[0], reply_lo[1])
+        near = dot_t(tables[2], amp_parts[0]) + dot_t(tables[0], amp_parts[2]) + dot_t(tables[1], amp_parts[1])
+        near = near + dot_t(tables[1], amp_parts[0]) + dot_t(tables[0], amp_parts[1])
+        near = near + dot_t(tables[0], amp_parts[0])
         for r in range(3):
             reply_out[1 + r] = near[r * n_dev : (r + 1) * n_dev]
 
@@ -463,10 +467,11 @@
 
     def sweep(it, carry):
         wait_reply(reply_in, reply_recv)
-        near_hi, near_lo = split(jnp.concatenate([reply_in[r] for r in (1, 2, 3)], axis=0))
+        near = jnp.concatenate([reply_in[r] for r in (1, 2, 3)], axis=0)
         lit = dot(from_lit[...], jnp.concatenate(split3(reply_in[0]), axis=1))
         lit = lit[:, :128] + lit[:, 128:256] + lit[:, 256:]
-        near = halves(dot(from_near[...], jnp.concatenate([near_hi, near_lo], axis=1)))
+        near = dot(from_near[...], jnp.concatenate(split3(near), axis=1))
+        near = near[:, :128] + near[:, 128:256] + near[:, 256:]
         wide = jnp.concatenate([lit * gain_mask[...], near * plain_mask[...]], axis=1)
         coeff = dot(wide.astype(BF16), fold).astype(BF16)
         gain = stamp_cols[:, 0:1]
@@ -478,26 +483,24 @@
             resid = pixels[i].astype(F32) - dot(coeff, both[i])
             weight = ROBUST / (resid * resid + softening)
             gram[...] += dot_t(weight.astype(BF16), pair[i])
-            proj[...] += dot_t((weight * resid).astype(BF16), wide_phi[i])
+            proj[...] += dot_t(both[i, 0:K, :], (weight * resid).astype(BF16))
 
         for i in range(n_chunk):
             one_chunk(i)
-        square = gain * gain
-        main_hi, main_lo = split(gram[:, :128] * square)
+        main_hi, main_lo = split(gram[:, :128] * (gain * gain))
         main = halves(dot(to_slot[...], jnp.concatenate([main_hi, main_lo], axis=1)))
-        rest = jnp.concatenate(
-            [proj[...] * gain_mask[...], gram[:, 128:] * (gain_mask[...] * gain)], axis=1
-        )
-        rest_hi, rest_lo = split(rest)
-        rest = dot(to_dest[...], rest_hi) + dot(to_dest[...], rest_lo)
+        proj_hi, proj_lo = split(jnp.concatenate([proj[...]] * CAP, axis=0) * gain_rows[...])
+        diag_hi, diag_lo = split(gram[:, 128:] * (gain_mask[...] * gain))
+        rest_proj = dot_t(to_dest[...], proj_hi) + dot_t(to_dest[...], proj_lo)
+        rest_diag = dot(to_dest[...], diag_hi) + dot(to_dest[...], diag_lo)
 
         @pl.when(it > 0)
         def _():
             wait_rows(rows_out, rows_send)
 
         rows_out[:, 0:CAP, :] = main.reshape(n_dev, CAP, 128)
-        rows_out[:, CAP, :] = rest[:, :128]
-        rows_out[:, CAP + 1, :] = rest[:, 128:]
+        rows_out[:, CAP, :] = rest_proj
+        rows_out[:, CAP + 1, :] = rest_diag
 
         def send(t):
             pltpu.make_async_remote_copy(
@@ -536,7 +539,10 @@
         sums_hi, sums_lo = split(sums + sums_in[it])
         full = dot_t(table_ref[...], sums_hi) + dot_t(table_ref[...], sums_lo)
         theta = theta_now[...]
-        theta = solve(full, jnp.exp(theta), theta, theta_ref[...])
+        step = solve(full, jnp.exp(theta), theta, theta_ref[...])
+        out_ref[0:K] = theta
+        out_ref[K:] = step
+        theta = theta + step
         theta_now[...] = theta
         wait_reply(reply_out, reply_send)
 
@@ -549,7 +555,6 @@
 
     lax.fori_loop(0, ITERS, sweep, 0)
     wait_rows(rows_out, rows_send)
-    out_ref[...] = theta_now[...]
 
 
 def local(
@@ -588,21 +593,21 @@
         pltpu.VMEM((8, 128), F32),
         pltpu.VMEM((n_chunk, n_stamp, chunk), BF16),
         pltpu.VMEM((n_chunk, 256, chunk), BF16),
-        pltpu.VMEM((n_chunk, 128, chunk), BF16),
         pltpu.VMEM((n_chunk, 32, chunk), BF16),
         pltpu.VMEM((n_stamp, 256), F32),
-        pltpu.VMEM((n_stamp, 128), F32),
+        pltpu.VMEM((K, n_stamp), F32),
         pltpu.VMEM((n_slot, n_stamp), BF16),
         pltpu.VMEM((n_dev, n_stamp), BF16),
         pltpu.VMEM((n_stamp, n_dev), BF16),
         pltpu.VMEM((n_stamp, 3 * n_dev), BF16),
         pltpu.VMEM((n_stamp, 128), F32),
+        pltpu.VMEM((128, n_stamp), F32),
         pltpu.VMEM((n_stamp, 128), F32),
         pltpu.VMEM((n_stamp, 128), F32),
         pltpu.VMEM((n_obj, n_slot), BF16),
         pltpu.VMEM((n_obj, n_slot), BF16),
         pltpu.VMEM((4 * n_dev, CAP * n_obj), BF16),
-        pltpu.VMEM((3 * n_dev, CAP * n_obj), BF16),
+        pltpu.VMEM((2, 3 * n_dev, CAP * n_obj), BF16),
         pltpu.VMEM((CAP * K, CAP * n_obj), BF16),
         pltpu.VMEM((3, CAP * K, CAP * n_obj), BF16),
         pltpu.VMEM((K, n_obj), F32),
@@ -628,9 +633,9 @@
         pltpu.SemaphoreType.DMA((ITERS,)),
         pltpu.SemaphoreType.DMA((ITERS,)),
     ]
-    return pl.pallas_call(
+    fitted = pl.pallas_call(
         functools.partial(kernel, (n_dev, n_stamp, n_obj, pix, chunk)),
-        out_shape=jax.ShapeDtypeStruct(theta_init.shape, F32),
+        out_shape=jax.ShapeDtypeStruct((2 * K, n_obj), F32),
         in_specs=[pl.BlockSpec(memory_space=pltpu.HBM)] * len(operands),
         out_specs=pl.BlockSpec(memory_space=pltpu.VMEM),
         scratch_shapes=scratch,
@@ -638,6 +643,7 @@
             collective_id=0, has_side_effects=True, vmem_limit_bytes=(64 << 20) - (1 << 16)
         ),
     )(*operands)
+    return fitted[:K] + fitted[K:]
 
 
 def solution(mesh):

time: 81.8 us -> 82.6 us (level)
  other arithmetic: 0 us -> 1.32 us
  local copies, waits for them, and re-layouts: 1.3 us -> 0 us
    add x0 -> x1, other arithmetic: none -> 1.32 us  [local(): return fitted[:K] + fitted[K:]]
    unnamed x1 -> x0, local copies, waits for them, and re-layouts: 1.3 us -> none
where the time goes in v3:
time: 82.6 us; the launch traced here: 82.4 us
  Pallas kernels  81.1 us (98%)
  other arithmetic  1.32 us (2%)
    pallas_call x1, Pallas kernels, local(): pl.pallas_call(functools.partial(kernel, (n_dev, n_stamp, n_obj, pix, chu...  81.1 us

profile of v3, /device:TPU:1, one launch (start us, length us, event | category | flops | bytes accessed | tf_op | source)
XLA Modules:
  0.0 82.4 jit_solution(2142835083953436754)
XLA Ops:
  0.0 81.1 %shard_map.109 = f32[32,64]{1,0:T(8,128)} custom-call(bf16[3,256,2304]{2,1,0:T(8,128)(2,1)} %bitcast.5, bf16[256]{0:T(256)(128)(2,1)} %gain_hbm.1, bf16[256]{0:T(256)(128)(2,1)} %invvar_hbm.1, s32[1,256]{1,0:T(1,128)} %bitcast.8, s32[1,256]{1,0:T(1,128)} %bitcast.9, bf16[3,16,2304]{2,1,0:T(8,128)(2,1)} %phi_hbm.1, bf16[3,16,2304]{2,1,0:T(8,128)(2,1)} %psi_hbm.1, ...), custom_call_target="tpu_custom_call" | custom-call | tf_op jit(solution)/shard_map/pallas_call | solution.py:636
  81.1 1.3 %slice_add_fusion = f32[16,64]{1,0:T(8,128)} fusion(f32[32,64]{1,0:T(8,128)} %shard_map.109), kind=kLoop, calls=%fused_computation | loop fusion | flops 1024 | bytes 12288 | tf_op jit(solution)/shard_map/add | solution.py:646

commit v4 on v3

--- a/solution.py
+++ b/solution.py
@@ -44,9 +44,21 @@
     return lax.dot_general(a, b, (((1,), (1,)), ((), ())), preferred_element_type=F32)
 
 
-def halves(x):
-    width = x.shape[1] // 2
-    return x[:, :width] + x[:, width:]
+def dot_exact(a, x):
+    width = x.shape[1]
+    sums = dot(a, jnp.concatenate(split3(x), axis=1))
+    return sums[:, :width] + (sums[:, width : 2 * width] + sums[:, 2 * width :])
+
+
+def dot_close(a, x):
+    width = x.shape[1]
+    sums = dot(a, jnp.concatenate(split(x), axis=1))
+    return sums[:, :width] + sums[:, width:]
+
+
+def dot_t_exact(a, x):
+    high, middle, low = split3(x)
+    return dot_t(a, high) + (dot_t(a, middle) + dot_t(a, low))
 
 
 def expand_table():
@@ -164,6 +176,7 @@
     reply_hi,
     reply_lo,
     reply_mask,
+    rest_mask,
     amp_parts,
     theta_now,
     meta_out,
@@ -435,6 +448,10 @@
 
     theta_now[...] = theta_ref[...]
     reply()
+    shape = (CAP * n_dev, 5 * 128)
+    rest_mask[...] = jnp.where(
+        iota(shape, 0) // n_dev == (iota(shape, 1) % 128) // K, 1.0, 0.0
+    ).astype(BF16)
     own_obj = meta_in[1]
     turned = dot_t(
         jnp.where(iota((128, 128), 0) == iota((128, 128), 1), 1.0, 0.0).astype(BF16), own_obj.astype(BF16)
@@ -468,10 +485,8 @@
     def sweep(it, carry):
         wait_reply(reply_in, reply_recv)
         near = jnp.concatenate([reply_in[r] for r in (1, 2, 3)], axis=0)
-        lit = dot(from_lit[...], jnp.concatenate(split3(reply_in[0]), axis=1))
-        lit = lit[:, :128] + lit[:, 128:256] + lit[:, 256:]
-        near = dot(from_near[...], jnp.concatenate(split3(near), axis=1))
-        near = near[:, :128] + near[:, 128:256] + near[:, 256:]
+        lit = dot_exact(from_lit[...], reply_in[0])
+        near = dot_exact(from_near[...], near)
         wide = jnp.concatenate([lit * gain_mask[...], near * plain_mask[...]], axis=1)
         coeff = dot(wide.astype(BF16), fold).astype(BF16)
         gain = stamp_cols[:, 0:1]
@@ -487,12 +502,9 @@
 
         for i in range(n_chunk):
             one_chunk(i)
-        main_hi, main_lo = split(gram[:, :128] * (gain * gain))
-        main = halves(dot(to_slot[...], jnp.concatenate([main_hi, main_lo], axis=1)))
-        proj_hi, proj_lo = split(jnp.concatenate([proj[...]] * CAP, axis=0) * gain_rows[...])
-        diag_hi, diag_lo = split(gram[:, 128:] * (gain_mask[...] * gain))
-        rest_proj = dot_t(to_dest[...], proj_hi) + dot_t(to_dest[...], proj_lo)
-        rest_diag = dot(to_dest[...], diag_hi) + dot(to_dest[...], diag_lo)
+        main = dot_close(to_slot[...], gram[:, :128] * (gain * gain))
+        rest_proj = dot_t_exact(to_dest[...], jnp.concatenate([proj[...]] * CAP, axis=0) * gain_rows[...])
+        rest_diag = dot_close(to_dest[...], gram[:, 128:] * (gain_mask[...] * gain))
 
         @pl.when(it > 0)
         def _():
@@ -516,14 +528,12 @@
         rows_in[me] = rows_out[me]
 
         wait_rows(rows_in, rows_recv)
-        slot_hi, slot_lo = split(rows_in[:, 0:CAP, :].reshape(n_slot, 128))
-        main_sum = halves(dot(member[...], jnp.concatenate([slot_hi, slot_lo], axis=1)))
-        rest = jnp.concatenate([rows_in[:, CAP, :], rows_in[:, CAP + 1, :]], axis=1)
-        rest = jnp.concatenate([rest] * CAP, axis=0)
-        shape = (CAP * n_dev, 256)
-        rest = jnp.where(iota(shape, 0) // n_dev == (iota(shape, 1) % 128) // K, rest, 0.0)
-        rest_hi, rest_lo = split(rest)
-        rest_sum = dot(member2[...], rest_hi) + dot(member2[...], rest_lo)
+        main_sum = dot_close(member[...], rows_in[:, 0:CAP, :].reshape(n_slot, 128))
+        parts = split3(rows_in[:, CAP, :]) + split(rows_in[:, CAP + 1, :])
+        parts = jnp.concatenate(parts, axis=1)
+        parts = dot(member2[...], jnp.concatenate([parts] * CAP, axis=0) * rest_mask[...])
+        proj_sum = parts[:, 0:128] + (parts[:, 128:256] + parts[:, 256:384])
+        rest_sum = jnp.concatenate([proj_sum, parts[:, 384:512] + parts[:, 512:640]], axis=1)
         sums = jnp.concatenate([main_sum, rest_sum], axis=1)
         sums_out[it] = sums
         copy = pltpu.make_async_remote_copy(
@@ -536,8 +546,7 @@
         )
         copy.start()
         copy.wait()
-        sums_hi, sums_lo = split(sums + sums_in[it])
-        full = dot_t(table_ref[...], sums_hi) + dot_t(table_ref[...], sums_lo)
+        full = dot_t_exact(table_ref[...], sums + sums_in[it])
         theta = theta_now[...]
         step = solve(full, jnp.exp(theta), theta, theta_ref[...])
         out_ref[0:K] = theta
@@ -609,6 +618,7 @@
         pltpu.VMEM((4 * n_dev, CAP * n_obj), BF16),
         pltpu.VMEM((2, 3 * n_dev, CAP * n_obj), BF16),
         pltpu.VMEM((CAP * K, CAP * n_obj), BF16),
+        pltpu.VMEM((CAP * n_dev, 5 * 128), BF16),
         pltpu.VMEM((3, CAP * K, CAP * n_obj), BF16),
         pltpu.VMEM((K, n_obj), F32),
         pltpu.VMEM((n_dev + 8, 128), F32),

time: 82.6 us -> 82.8 us (level)
  no operation moved by 1% of the time
where the time goes in v4:
time: 82.8 us; the launch traced here: 82.7 us
  Pallas kernels  81.3 us (98%)
  other arithmetic  1.32 us (2%)
    pallas_call x1, Pallas kernels, local(): pl.pallas_call(functools.partial(kernel, (n_dev, n_stamp, n_obj, pix, chu...  81.3 us

profile of v4, /device:TPU:1, one launch (start us, length us, event | category | flops | bytes accessed | tf_op | source)
XLA Modules:
  0.0 82.7 jit_solution(14572590202808398939)
XLA Ops:
  0.0 81.3 %shard_map.109 = f32[32,64]{1,0:T(8,128)} custom-call(bf16[3,256,2304]{2,1,0:T(8,128)(2,1)} %bitcast.5, bf16[256]{0:T(256)(128)(2,1)} %gain_hbm.1, bf16[256]{0:T(256)(128)(2,1)} %invvar_hbm.1, s32[1,256]{1,0:T(1,128)} %bitcast.8, s32[1,256]{1,0:T(1,128)} %bitcast.9, bf16[3,16,2304]{2,1,0:T(8,128)(2,1)} %phi_hbm.1, bf16[3,16,2304]{2,1,0:T(8,128)(2,1)} %psi_hbm.1, ...), custom_call_target="tpu_custom_call" | custom-call | tf_op jit(solution)/shard_map/pallas_call | solution.py:646
  81.3 1.3 %slice_add_fusion = f32[16,64]{1,0:T(8,128)} fusion(f32[32,64]{1,0:T(8,128)} %shard_map.109), kind=kLoop, calls=%fused_computation | loop fusion | flops 1024 | bytes 12288 | tf_op jit(solution)/shard_map/add | solution.py:656

commit v5 on v4

--- a/solution.py
+++ b/solution.py
@@ -382,7 +382,7 @@
         twice = jnp.concatenate(
             [jnp.concatenate([blend, zero], axis=1), jnp.concatenate([zero, blend], axis=1)], axis=0
         )
-        return jnp.concatenate(split3(twice), axis=0)
+        return jnp.concatenate(split(twice), axis=0)
 
     blends = [None, blend_of(nb_ref[...]), None]
     for copy in nb_copies:
@@ -410,18 +410,15 @@
             own = weights[i * n_dev : (i + 1) * n_dev]
             columns = slice(i * 2 * n_obj, (i + 1) * 2 * n_obj)
             reply_hi[at : at + n_dev, columns] = own[:, : 2 * n_obj]
-            reply_lo[0, at - n_dev : at, columns] = own[:, 2 * n_obj : 4 * n_obj]
-            reply_lo[1, at - n_dev : at, columns] = own[:, 4 * n_obj :]
+            reply_lo[at - n_dev : at, columns] = own[:, 2 * n_obj :]
 
     def reply():
         for part in range(3):
             term = dot_t(reply_hi[0:n_dev, :], amp_parts[part])
             lit = term if part == 0 else lit + term
         reply_out[0] = lit
-        tables = (reply_hi[n_dev:, :], reply_lo[0], reply_lo[1])
-        near = dot_t(tables[2], amp_parts[0]) + dot_t(tables[0], amp_parts[2]) + dot_t(tables[1], amp_parts[1])
-        near = near + dot_t(tables[1], amp_parts[0]) + dot_t(tables[0], amp_parts[1])
-        near = near + dot_t(tables[0], amp_parts[0])
+        near = dot_t(reply_hi[n_dev:, :], amp_parts[1]) + dot_t(reply_lo[...], amp_parts[0])
+        near = near + dot_t(reply_hi[n_dev:, :], amp_parts[0])
         for r in range(3):
             reply_out[1 + r] = near[r * n_dev : (r + 1) * n_dev]
 
@@ -486,7 +483,7 @@
         wait_reply(reply_in, reply_recv)
         near = jnp.concatenate([reply_in[r] for r in (1, 2, 3)], axis=0)
         lit = dot_exact(from_lit[...], reply_in[0])
-        near = dot_exact(from_near[...], near)
+        near = dot_close(from_near[...], near)
         wide = jnp.concatenate([lit * gain_mask[...], near * plain_mask[...]], axis=1)
         coeff = dot(wide.astype(BF16), fold).astype(BF16)
         gain = stamp_cols[:, 0:1]
@@ -616,7 +613,7 @@
         pltpu.VMEM((n_obj, n_slot), BF16),
         pltpu.VMEM((n_obj, n_slot), BF16),
         pltpu.VMEM((4 * n_dev, CAP * n_obj), BF16),
-        pltpu.VMEM((2, 3 * n_dev, CAP * n_obj), BF16),
+        pltpu.VMEM((3 * n_dev, CAP * n_obj), BF16),
         pltpu.VMEM((CAP * K, CAP * n_obj), BF16),
         pltpu.VMEM((CAP * n_dev, 5 * 128), BF16),
         pltpu.VMEM((3, CAP * K, CAP * n_obj), BF16),

time: 82.8 us -> 82.1 us (level)
  no operation moved by 1% of the time
where the time goes in v5:
time: 82.1 us; the launch traced here: 81.9 us
  Pallas kernels  80.6 us (98%)
  other arithmetic  1.32 us (2%)
    pallas_call x1, Pallas kernels, local(): pl.pallas_call(functools.partial(kernel, (n_dev, n_stamp, n_obj, pix, chu...  80.6 us

profile of v5, /device:TPU:1, one launch (start us, length us, event | category | flops | bytes accessed | tf_op | source)
XLA Modules:
  0.0 81.9 jit_solution(9050327209687764175)
XLA Ops:
  0.0 80.6 %shard_map.109 = f32[32,64]{1,0:T(8,128)} custom-call(bf16[3,256,2304]{2,1,0:T(8,128)(2,1)} %bitcast.5, bf16[256]{0:T(256)(128)(2,1)} %gain_hbm.1, bf16[256]{0:T(256)(128)(2,1)} %invvar_hbm.1, s32[1,256]{1,0:T(1,128)} %bitcast.8, s32[1,256]{1,0:T(1,128)} %bitcast.9, bf16[3,16,2304]{2,1,0:T(8,128)(2,1)} %phi_hbm.1, bf16[3,16,2304]{2,1,0:T(8,128)(2,1)} %psi_hbm.1, ...), custom_call_target="tpu_custom_call" | custom-call | tf_op jit(solution)/shard_map/pallas_call | solution.py:643
  80.6 1.3 %slice_add_fusion = f32[16,64]{1,0:T(8,128)} fusion(f32[32,64]{1,0:T(8,128)} %shard_map.109), kind=kLoop, calls=%fused_computation | loop fusion | flops 1024 | bytes 12288 | tf_op jit(solution)/shard_map/add | solution.py:653

commit v6 on v5

--- a/solution.py
+++ b/solution.py
@@ -229,14 +229,6 @@
 
             lax.fori_loop(1, n_dev, step, 0)
 
-    barrier = pltpu.get_barrier_semaphore()
-
-    def greet(t):
-        pl.semaphore_signal(barrier, inc=1, device_id=(t, core), device_id_type=MESH)
-
-    each_peer(greet)
-    pl.semaphore_signal(barrier, inc=1, device_id=(me, 1 - core), device_id_type=MESH)
-
     in_copies = []
     for i, (src, dst) in enumerate(
         (
@@ -255,6 +247,14 @@
         copy = pltpu.make_async_copy(src, dst, in_sem.at[i])
         copy.start()
         in_copies.append(copy)
+    barrier = pltpu.get_barrier_semaphore()
+
+    def greet(t):
+        pl.semaphore_signal(barrier, inc=1, device_id=(t, core), device_id_type=MESH)
+
+    each_peer(greet)
+    pl.semaphore_signal(barrier, inc=1, device_id=(me, 1 - core), device_id_type=MESH)
+
     pixel_copies = []
     for i in range(n_chunk):
         band, part = divmod(i, per_band)

time: 82.1 us -> 82.1 us (level)
  no operation moved by 1% of the time
where the time goes in v6:
time: 82.1 us; the launch traced here: 82 us
  Pallas kernels  80.6 us (98%)
  other arithmetic  1.32 us (2%)
    pallas_call x1, Pallas kernels, local(): pl.pallas_call(functools.partial(kernel, (n_dev, n_stamp, n_obj, pix, chu...  80.6 us

profile of v6, /device:TPU:1, one launch (start us, length us, event | category | flops | bytes accessed | tf_op | source)
XLA Modules:
  0.0 82.0 jit_solution(6243992065469947205)
XLA Ops:
  0.0 80.6 %shard_map.109 = f32[32,64]{1,0:T(8,128)} custom-call(bf16[3,256,2304]{2,1,0:T(8,128)(2,1)} %bitcast.5, bf16[256]{0:T(256)(128)(2,1)} %gain_hbm.1, bf16[256]{0:T(256)(128)(2,1)} %invvar_hbm.1, s32[1,256]{1,0:T(1,128)} %bitcast.8, s32[1,256]{1,0:T(1,128)} %bitcast.9, bf16[3,16,2304]{2,1,0:T(8,128)(2,1)} %phi_hbm.1, bf16[3,16,2304]{2,1,0:T(8,128)(2,1)} %psi_hbm.1, ...), custom_call_target="tpu_custom_call" | custom-call | tf_op jit(solution)/shard_map/pallas_call | solution.py:643
  80.7 1.3 %slice_add_fusion = f32[16,64]{1,0:T(8,128)} fusion(f32[32,64]{1,0:T(8,128)} %shard_map.109), kind=kLoop, calls=%fused_computation | loop fusion | flops 1024 | bytes 12288 | tf_op jit(solution)/shard_map/add | solution.py:653
